TPU v7x, 32 devices: a whole 2x2x4 slice. The times are simulated.
32 devices in a mesh: grp: 2 (over y), chan: 4 (over x, core), tm: 4 (over z).
Axes of the slice: x: 2, y: 2, z: 4, core: 2. Of those that a mesh axis runs over, the one named last changes fastest.
Arguments:
- spectra: bfloat16 [4096, 128, 128], P(('grp', 'chan'), 'tm'), parts along dimension 0, may hold values from -6 to 6
- band_width: int32 [8], P(('grp', 'chan')), parts along dimension 0, may hold values from 512 to 1024, as said below
- pair_list: int32 [2, 32768], P(None, ('grp', 'chan')), parts along dimension 1, may hold values from 0 to 1023, as said below
- owner_ids: int32 [32768], P(('grp', 'chan')), parts along dimension 0, may hold values from 0 to 3, as said below
Outputs:
- stacks: float32 [65536, 128], P(('grp', 'chan', 'tm')), parts along dimension 0
There are 2 independent parts, one for each index of `grp`. A program takes and returns all parts, laid end to end along the dimension named above; each array names one. Nothing has to cross between parts.
Inputs may be any that keep to these rules, and one draw needn't show every extreme that they name: `band_width`: one block has a band of exactly 1024. `pair_list`: row 0 is below 512; row 1 is below the band of the pair's block; some pair reaches its block's band minus one. `owner_ids`: among the 4096 pairs of one block no owner appears more than 2048 times, and one owner exactly 2048 times.
All inputs are finite; a program needn't handle non-finite values.
Results may differ from a plain program's by a relative error of at most 0.0003.
Values may be sent and summed in bfloat16 or wider, within the bound.
A program may use at most 128 MiB of HBM per device.

v0:
```python
import math

import jax
import jax.numpy as jnp
from jax import lax
from jax.sharding import PartitionSpec as P

K_SH = 2


def from_behind(block, axis, distance):
    devices = range(lax.axis_size(axis))
    route = [((i - distance) % len(devices), i) for i in devices]
    return lax.ppermute(block, axis, route)


def inverse_table(half_bins):
    length = 2 * half_bins
    row_ids = lax.iota(jnp.int32, length)
    frequency = row_ids % half_bins
    lag_ids = lax.iota(jnp.int32, length)
    phases = (frequency[:, None] * lag_ids[None, :] % length).astype(jnp.float32) * (
        2.0 * math.pi / length
    )
    weights = jnp.where(frequency == 0, 1.0, 2.0).astype(jnp.float32)[:, None]
    return jnp.where(
        (row_ids >= half_bins)[:, None], -weights * jnp.sin(phases), weights * jnp.cos(phases)
    )


def pair_spectra(source_rows, receiver_rows, half_bins):
    source_re = source_rows[..., :half_bins]
    source_im = source_rows[..., half_bins:]
    receiver_re = receiver_rows[..., :half_bins]
    receiver_im = receiver_rows[..., half_bins:]
    real_part = jnp.einsum(
        "pwf,pwf->pf", source_re, receiver_re, preferred_element_type=jnp.float32
    ) + jnp.einsum("pwf,pwf->pf", source_im, receiver_im, preferred_element_type=jnp.float32)
    imag_part = jnp.einsum(
        "pwf,pwf->pf", source_im, receiver_re, preferred_element_type=jnp.float32
    ) - jnp.einsum("pwf,pwf->pf", source_re, receiver_im, preferred_element_type=jnp.float32)
    return jnp.concatenate([real_part, imag_part], axis=1)


def slot_numbers(owner_ids, tm_size):
    npairs = owner_ids.shape[0]
    width_block = math.gcd(npairs, 256)
    count_blocks = npairs // width_block
    onehot = (owner_ids[:, None] == jnp.arange(tm_size, dtype=jnp.int32)[None, :]).astype(
        jnp.float32
    )
    grouped = onehot.reshape(count_blocks, width_block, tm_size)
    row_ids = lax.iota(jnp.int32, width_block)
    lower = (row_ids[:, None] >= row_ids[None, :]).astype(jnp.float32)
    within = jnp.einsum("ij,njt->nit", lower, grouped, precision=lax.Precision.HIGHEST)
    totals = within[:, -1, :]
    before = jnp.cumsum(totals, axis=0) - totals
    ranking = (within + before[:, None, :] - 1.0).reshape(npairs, tm_size)
    return jnp.sum(ranking * onehot, axis=1).astype(jnp.int32)


def shards(spectra, band_width, pair_list, owner_ids):
    half_bins = spectra.shape[2] // 2
    length = 2 * half_bins
    channel_rows = spectra.shape[0]
    window_rows = spectra.shape[1]
    npairs = pair_list.shape[1]
    tm_size = lax.axis_size("tm")
    capacity = 2 * npairs // tm_size
    windows = window_rows * tm_size
    blocks = [spectra]
    current = spectra
    for shift_count in range(K_SH):
        current = from_behind(current, "chan", -1)
        blocks.append(current)
    nearby = jnp.concatenate(blocks, axis=0).reshape(-1, window_rows * length)
    own_rows = spectra.reshape(channel_rows, window_rows * length)
    sources = pair_list[0]
    offsets = pair_list[1]
    receivers = sources + offsets
    group_size = math.gcd(npairs, 512)

    def cross_block(indices):
        source_ids, receiver_ids = indices
        source_rows = jnp.take(own_rows, source_ids, axis=0).reshape(
            group_size, window_rows, length
        )
        receiver_rows = jnp.take(nearby, receiver_ids, axis=0).reshape(
            group_size, window_rows, length
        )
        return pair_spectra(source_rows, receiver_rows, half_bins)

    cross_sums = lax.map(
        cross_block, (sources.reshape(-1, group_size), receivers.reshape(-1, group_size))
    ).reshape(npairs, length)
    tapering = (1.0 - offsets.astype(jnp.float32) / band_width[0].astype(jnp.float32)) / windows
    slot_ids = slot_numbers(owner_ids, tm_size)
    targets = owner_ids * capacity + slot_ids
    slot_pairs = (
        jnp.full((tm_size * capacity,), npairs, jnp.int32)
        .at[targets]
        .set(lax.iota(jnp.int32, npairs))
    )
    table_values = inverse_table(half_bins)
    weighted = (
        jnp.dot(cross_sums, table_values, precision=lax.Precision.HIGHEST) * tapering[:, None]
    )
    buffer = jnp.take(weighted, slot_pairs, axis=0, mode="fill", fill_value=0.0)
    return lax.psum_scatter(buffer, "tm", scatter_dimension=0, tiled=True)


def solution(mesh):
    return jax.shard_map(
        shards,
        mesh=mesh,
        in_specs=(
            P(("grp", "chan"), "tm", None),
            P(("grp", "chan")),
            P(None, ("grp", "chan")),
            P(("grp", "chan")),
        ),
        out_specs=P(("grp", "chan", "tm"), None),
        check_vma=False,
    )
```

profile of v0, /device:TPU:0, one launch (start us, length us, event | category | flops | bytes accessed | tf_op | source)
XLA Modules:
  0.0 628.8 jit_solution(4734600489120873812)
XLA Ops:
  6.5 2.4 collective-permute-start
  8.9 46.3 %collective-permute-done = bf16[512,32,128]{2,1,0:T(8,128)(2,1)} collective-permute-done((bf16[512,32,128]{2,1,0:T(8,128)(2,1)}, bf16[512,32,128]{2,1,0:T(8,128)(2,1)}, u32[]{:S(2)}, u32[]{:S(2)}) %collective-permute-start) | collective-permute-done | bytes 4194336 | tf_op jit(solution)/shard_map/ppermute | solution.py:14
  58.1 8.3 %copy.45 = bf16[64,8,32,128]{3,1,2,0:T(8,128)(2,1)} copy(bf16[64,8,32,128]{3,2,1,0:T(8,128)(2,1)} %bitcast.96) | data formatting | bytes 8388608
  68.2 15.5 %scatter_custom_fusion = s32[8192]{0:T(1024)S(1)} fusion(s32[4096]{0:T(1024)S(1)} %compare_select_fusion.5, s32[4096]{0:T(1024)S(1)} %iota.38, s32[]{:T(128)} %constant.97.clone.1), kind=kCustom, calls=%fused_computation.71 | custom fusion | bytes 32772 | tf_op jit(solution)/shard_map/scatter | solution.py:102
  87.2 16.3 %collective-permute-done.1 = bf16[512,32,128]{2,1,0:T(8,128)(2,1)} collective-permute-done((bf16[512,32,128]{2,1,0:T(8,128)(2,1)}, bf16[512,32,128]{2,1,0:T(8,128)(2,1)}, u32[]{:S(2)}, u32[]{:S(2)}) %collective-permute-start.1) | collective-permute-done | bytes 4194336 | tf_op jit(solution)/shard_map/ppermute | solution.py:14
  103.5 10.3 %pad_maximum_fusion = bf16[1536,32,128]{2,1,0:T(8,128)(2,1)S(1)} fusion(bf16[512,32,128]{2,1,0:T(8,128)(2,1)} %collective-permute-done.1, bf16[512,32,128]{2,1,0:T(8,128)(2,1)} %collective-permute-done, bf16[512,32,128]{2,1,0:T(8,128)(2,1)} %param.6), kind=kLoop, calls=%fused_computation.31 | loop fusion | flops 12582912 | bytes 25165824 | tf_op jit(solution)/shard_map/concatenate | solution.py:76
  113.9 8.6 %copy.44 = bf16[192,8,32,128]{3,1,2,0:T(8,128)(2,1)} copy(bf16[192,8,32,128]{3,2,1,0:T(8,128)(2,1)S(1)} %bitcast.95) | data formatting | bytes 25165824
  122.5 381.9 %while.10 = (s32[]{:T(128)}, f32[8,512,128]{2,1,0:T(8,128)}, s32[8,512]{1,0:T(8,128)S(1)}, bf16[512,4096]{1,0:T(8,128)(2,1)}, s32[8,512]{1,0:T(8,128)S(1)}, /*index=5*/bf16[1536,4096]{1,0:T(8,128)(2,1)}, s32[]{:T(128)}) while((s32[]{:T(128)}, f32[8,512,128]{2,1,0:T(8,128)}, s32[8,512]{1,0:T(8,128)S(1)}, bf16[512,4096]{1,0:T(8,128)(2,1)}, ...), condition=%wide.region_4.5_spmd, body=%wide.region_3.4_spmd.sunk | while | flops 16788480 | bytes 77367408 | solution.py:93
  122.7 11.3 %gather_fusion = bf16[512,4096]{1,0:T(8,128)(2,1)} fusion(bf16[512,4096]{1,0:T(8,128)(2,1)} %get-tuple-element.134, s32[1024]{0:T(1024)S(1)} %pad_clamp_fusion.4), kind=kCustom, calls=%fused_computation.clone.1 | custom fusion | bytes 8390656 | tf_op jit(solution)/shard_map/while/body/eval_jaxpr/jit(_take)/gather | solution.py:85
  134.0 3.4 copy.48
  137.4 3.2 bitcast_select_fusion.4
  140.7 14.8 %gather_fusion.1 = bf16[512,4096]{1,0:T(8,128)(2,1)} fusion(bf16[1536,4096]{1,0:T(8,128)(2,1)} %get-tuple-element.136, s32[1024]{0:T(1024)S(1)} %pad_clamp_fusion.5), kind=kCustom, calls=%fused_computation.1.clone.1 | custom fusion | bytes 8390656 | tf_op jit(solution)/shard_map/while/body/eval_jaxpr/jit(_take)/gather | solution.py:88
  155.5 3.4 copy.49
  158.9 2.0 bitcast_select_fusion.5
  161.1 8.3 %fusion.43 = (f32[512,64]{1,0:T(8,128)S(1)}, f32[512,64]{1,0:T(8,128)S(1)}, f32[512,64]{1,0:T(8,128)S(1)}, f32[512,64]{1,0:T(8,128)S(1)}) fusion(bf16[512,32,128]{2,1,0:T(8,128)(2,1)S(1)} %copy-done, bf16[512,32,128]{2,1,0:T(8,128)(2,1)S(1)} %bitcast_select_fusion.5), kind=kLoop, calls=%fused_computation.10.clone.1 | loop fusion | flops 12451840 | bytes 8912896 | tf_op jit(solution)/shard_map/while/body/eval_jaxpr/pwf,pwf->pf/dot_general | solution.py:38
  170.4 11.3 %gather_fusion = bf16[512,4096]{1,0:T(8,128)(2,1)} fusion(bf16[512,4096]{1,0:T(8,128)(2,1)} %get-tuple-element.134, s32[1024]{0:T(1024)S(1)} %pad_clamp_fusion.4), kind=kCustom, calls=%fused_computation.clone.1 | custom fusion | bytes 8390656 | tf_op jit(solution)/shard_map/while/body/eval_jaxpr/jit(_take)/gather | solution.py:85
  181.7 3.4 copy.48
  185.1 3.2 bitcast_select_fusion.4
  188.4 14.8 %gather_fusion.1 = bf16[512,4096]{1,0:T(8,128)(2,1)} fusion(bf16[1536,4096]{1,0:T(8,128)(2,1)} %get-tuple-element.136, s32[1024]{0:T(1024)S(1)} %pad_clamp_fusion.5), kind=kCustom, calls=%fused_computation.1.clone.1 | custom fusion | bytes 8390656 | tf_op jit(solution)/shard_map/while/body/eval_jaxpr/jit(_take)/gather | solution.py:88
  203.2 3.4 copy.49
  206.6 2.0 bitcast_select_fusion.5
  208.8 8.3 %fusion.43 = (f32[512,64]{1,0:T(8,128)S(1)}, f32[512,64]{1,0:T(8,128)S(1)}, f32[512,64]{1,0:T(8,128)S(1)}, f32[512,64]{1,0:T(8,128)S(1)}) fusion(bf16[512,32,128]{2,1,0:T(8,128)(2,1)S(1)} %copy-done, bf16[512,32,128]{2,1,0:T(8,128)(2,1)S(1)} %bitcast_select_fusion.5), kind=kLoop, calls=%fused_computation.10.clone.1 | loop fusion | flops 12451840 | bytes 8912896 | tf_op jit(solution)/shard_map/while/body/eval_jaxpr/pwf,pwf->pf/dot_general | solution.py:38
  218.1 11.3 %gather_fusion = bf16[512,4096]{1,0:T(8,128)(2,1)} fusion(bf16[512,4096]{1,0:T(8,128)(2,1)} %get-tuple-element.134, s32[1024]{0:T(1024)S(1)} %pad_clamp_fusion.4), kind=kCustom, calls=%fused_computation.clone.1 | custom fusion | bytes 8390656 | tf_op jit(solution)/shard_map/while/body/eval_jaxpr/jit(_take)/gather | solution.py:85
  229.4 3.4 copy.48
  232.8 3.2 bitcast_select_fusion.4
  236.1 14.8 %gather_fusion.1 = bf16[512,4096]{1,0:T(8,128)(2,1)} fusion(bf16[1536,4096]{1,0:T(8,128)(2,1)} %get-tuple-element.136, s32[1024]{0:T(1024)S(1)} %pad_clamp_fusion.5), kind=kCustom, calls=%fused_computation.1.clone.1 | custom fusion | bytes 8390656 | tf_op jit(solution)/shard_map/while/body/eval_jaxpr/jit(_take)/gather | solution.py:88
  250.9 3.4 copy.49
  256.5 8.3 %fusion.43 = (f32[512,64]{1,0:T(8,128)S(1)}, f32[512,64]{1,0:T(8,128)S(1)}, f32[512,64]{1,0:T(8,128)S(1)}, f32[512,64]{1,0:T(8,128)S(1)}) fusion(bf16[512,32,128]{2,1,0:T(8,128)(2,1)S(1)} %copy-done, bf16[512,32,128]{2,1,0:T(8,128)(2,1)S(1)} %bitcast_select_fusion.5), kind=kLoop, calls=%fused_computation.10.clone.1 | loop fusion | flops 12451840 | bytes 8912896 | tf_op jit(solution)/shard_map/while/body/eval_jaxpr/pwf,pwf->pf/dot_general | solution.py:38
  265.8 11.3 %gather_fusion = bf16[512,4096]{1,0:T(8,128)(2,1)} fusion(bf16[512,4096]{1,0:T(8,128)(2,1)} %get-tuple-element.134, s32[1024]{0:T(1024)S(1)} %pad_clamp_fusion.4), kind=kCustom, calls=%fused_computation.clone.1 | custom fusion | bytes 8390656 | tf_op jit(solution)/shard_map/while/body/eval_jaxpr/jit(_take)/gather | solution.py:85
  277.1 3.4 copy.48
  280.6 3.2 bitcast_select_fusion.4
  283.8 14.8 %gather_fusion.1 = bf16[512,4096]{1,0:T(8,128)(2,1)} fusion(bf16[1536,4096]{1,0:T(8,128)(2,1)} %get-tuple-element.136, s32[1024]{0:T(1024)S(1)} %pad_clamp_fusion.5), kind=kCustom, calls=%fused_computation.1.clone.1 | custom fusion | bytes 8390656 | tf_op jit(solution)/shard_map/while/body/eval_jaxpr/jit(_take)/gather | solution.py:88
  298.6 3.4 copy.49
  302.1 2.0 bitcast_select_fusion.5
  304.2 8.3 %fusion.43 = (f32[512,64]{1,0:T(8,128)S(1)}, f32[512,64]{1,0:T(8,128)S(1)}, f32[512,64]{1,0:T(8,128)S(1)}, f32[512,64]{1,0:T(8,128)S(1)}) fusion(bf16[512,32,128]{2,1,0:T(8,128)(2,1)S(1)} %copy-done, bf16[512,32,128]{2,1,0:T(8,128)(2,1)S(1)} %bitcast_select_fusion.5), kind=kLoop, calls=%fused_computation.10.clone.1 | loop fusion | flops 12451840 | bytes 8912896 | tf_op jit(solution)/shard_map/while/body/eval_jaxpr/pwf,pwf->pf/dot_general | solution.py:38
  313.5 11.3 %gather_fusion = bf16[512,4096]{1,0:T(8,128)(2,1)} fusion(bf16[512,4096]{1,0:T(8,128)(2,1)} %get-tuple-element.134, s32[1024]{0:T(1024)S(1)} %pad_clamp_fusion.4), kind=kCustom, calls=%fused_computation.clone.1 | custom fusion | bytes 8390656 | tf_op jit(solution)/shard_map/while/body/eval_jaxpr/jit(_take)/gather | solution.py:85
  324.8 3.4 copy.48
  328.3 3.2 bitcast_select_fusion.4
  331.5 14.8 %gather_fusion.1 = bf16[512,4096]{1,0:T(8,128)(2,1)} fusion(bf16[1536,4096]{1,0:T(8,128)(2,1)} %get-tuple-element.136, s32[1024]{0:T(1024)S(1)} %pad_clamp_fusion.5), kind=kCustom, calls=%fused_computation.1.clone.1 | custom fusion | bytes 8390656 | tf_op jit(solution)/shard_map/while/body/eval_jaxpr/jit(_take)/gather | solution.py:88
  346.3 3.4 copy.49
  352.0 8.3 %fusion.43 = (f32[512,64]{1,0:T(8,128)S(1)}, f32[512,64]{1,0:T(8,128)S(1)}, f32[512,64]{1,0:T(8,128)S(1)}, f32[512,64]{1,0:T(8,128)S(1)}) fusion(bf16[512,32,128]{2,1,0:T(8,128)(2,1)S(1)} %copy-done, bf16[512,32,128]{2,1,0:T(8,128)(2,1)S(1)} %bitcast_select_fusion.5), kind=kLoop, calls=%fused_computation.10.clone.1 | loop fusion | flops 12451840 | bytes 8912896 | tf_op jit(solution)/shard_map/while/body/eval_jaxpr/pwf,pwf->pf/dot_general | solution.py:38
  361.3 11.3 %gather_fusion = bf16[512,4096]{1,0:T(8,128)(2,1)} fusion(bf16[512,4096]{1,0:T(8,128)(2,1)} %get-tuple-element.134, s32[1024]{0:T(1024)S(1)} %pad_clamp_fusion.4), kind=kCustom, calls=%fused_computation.clone.1 | custom fusion | bytes 8390656 | tf_op jit(solution)/shard_map/while/body/eval_jaxpr/jit(_take)/gather | solution.py:85
  372.5 3.4 copy.48
  376.0 3.2 bitcast_select_fusion.4
  379.2 14.8 %gather_fusion.1 = bf16[512,4096]{1,0:T(8,128)(2,1)} fusion(bf16[1536,4096]{1,0:T(8,128)(2,1)} %get-tuple-element.136, s32[1024]{0:T(1024)S(1)} %pad_clamp_fusion.5), kind=kCustom, calls=%fused_computation.1.clone.1 | custom fusion | bytes 8390656 | tf_op jit(solution)/shard_map/while/body/eval_jaxpr/jit(_take)/gather | solution.py:88
  394.0 3.4 copy.49
  399.7 8.3 %fusion.43 = (f32[512,64]{1,0:T(8,128)S(1)}, f32[512,64]{1,0:T(8,128)S(1)}, f32[512,64]{1,0:T(8,128)S(1)}, f32[512,64]{1,0:T(8,128)S(1)}) fusion(bf16[512,32,128]{2,1,0:T(8,128)(2,1)S(1)} %copy-done, bf16[512,32,128]{2,1,0:T(8,128)(2,1)S(1)} %bitcast_select_fusion.5), kind=kLoop, calls=%fused_computation.10.clone.1 | loop fusion | flops 12451840 | bytes 8912896 | tf_op jit(solution)/shard_map/while/body/eval_jaxpr/pwf,pwf->pf/dot_general | solution.py:38
  409.0 11.3 %gather_fusion = bf16[512,4096]{1,0:T(8,128)(2,1)} fusion(bf16[512,4096]{1,0:T(8,128)(2,1)} %get-tuple-element.134, s32[1024]{0:T(1024)S(1)} %pad_clamp_fusion.4), kind=kCustom, calls=%fused_computation.clone.1 | custom fusion | bytes 8390656 | tf_op jit(solution)/shard_map/while/body/eval_jaxpr/jit(_take)/gather | solution.py:85
  420.3 3.4 copy.48
  423.7 3.2 bitcast_select_fusion.4
  427.0 14.8 %gather_fusion.1 = bf16[512,4096]{1,0:T(8,128)(2,1)} fusion(bf16[1536,4096]{1,0:T(8,128)(2,1)} %get-tuple-element.136, s32[1024]{0:T(1024)S(1)} %pad_clamp_fusion.5), kind=kCustom, calls=%fused_computation.1.clone.1 | custom fusion | bytes 8390656 | tf_op jit(solution)/shard_map/while/body/eval_jaxpr/jit(_take)/gather | solution.py:88
  441.8 3.4 copy.49
  445.2 2.0 bitcast_select_fusion.5
  447.4 8.3 %fusion.43 = (f32[512,64]{1,0:T(8,128)S(1)}, f32[512,64]{1,0:T(8,128)S(1)}, f32[512,64]{1,0:T(8,128)S(1)}, f32[512,64]{1,0:T(8,128)S(1)}) fusion(bf16[512,32,128]{2,1,0:T(8,128)(2,1)S(1)} %copy-done, bf16[512,32,128]{2,1,0:T(8,128)(2,1)S(1)} %bitcast_select_fusion.5), kind=kLoop, calls=%fused_computation.10.clone.1 | loop fusion | flops 12451840 | bytes 8912896 | tf_op jit(solution)/shard_map/while/body/eval_jaxpr/pwf,pwf->pf/dot_general | solution.py:38
  456.7 11.3 %gather_fusion = bf16[512,4096]{1,0:T(8,128)(2,1)} fusion(bf16[512,4096]{1,0:T(8,128)(2,1)} %get-tuple-element.134, s32[1024]{0:T(1024)S(1)} %pad_clamp_fusion.4), kind=kCustom, calls=%fused_computation.clone.1 | custom fusion | bytes 8390656 | tf_op jit(solution)/shard_map/while/body/eval_jaxpr/jit(_take)/gather | solution.py:85
  468.0 3.4 copy.48
  471.4 3.2 bitcast_select_fusion.4
  474.7 14.8 %gather_fusion.1 = bf16[512,4096]{1,0:T(8,128)(2,1)} fusion(bf16[1536,4096]{1,0:T(8,128)(2,1)} %get-tuple-element.136, s32[1024]{0:T(1024)S(1)} %pad_clamp_fusion.5), kind=kCustom, calls=%fused_computation.1.clone.1 | custom fusion | bytes 8390656 | tf_op jit(solution)/shard_map/while/body/eval_jaxpr/jit(_take)/gather | solution.py:88
  489.5 3.4 copy.49
  495.1 8.3 %fusion.43 = (f32[512,64]{1,0:T(8,128)S(1)}, f32[512,64]{1,0:T(8,128)S(1)}, f32[512,64]{1,0:T(8,128)S(1)}, f32[512,64]{1,0:T(8,128)S(1)}) fusion(bf16[512,32,128]{2,1,0:T(8,128)(2,1)S(1)} %copy-done, bf16[512,32,128]{2,1,0:T(8,128)(2,1)S(1)} %bitcast_select_fusion.5), kind=kLoop, calls=%fused_computation.10.clone.1 | loop fusion | flops 12451840 | bytes 8912896 | tf_op jit(solution)/shard_map/while/body/eval_jaxpr/pwf,pwf->pf/dot_general | solution.py:38
  504.4 3.7 convolution_multiply_fusion
  508.1 27.7 %gather_fusion.2 = f32[8192,128]{1,0:T(8,128)} fusion(f32[4096,128]{1,0:T(8,128)S(1)} %convolution_multiply_fusion, s32[8192]{0:T(1024)S(1)} %copy-done.1), kind=kCustom, calls=%fused_computation.2 | custom fusion | bytes 8421376 | tf_op jit(solution)/shard_map/jit(_take)/gather | solution.py:108
  535.8 7.5 %broadcast_select_fusion = f32[8192,128]{1,0:T(8,128)} fusion(f32[8192,128]{1,0:T(8,128)} %gather_fusion.2, pred[8192]{0:T(1024)(128)(4,1)S(1)} %copy-done.5), kind=kLoop, calls=%fused_computation.34 | loop fusion | flops 1048576 | bytes 8396800 | tf_op jit(solution)/shard_map/jit(_take)/select_n | solution.py:108
  543.3 78.6 %reduce-scatter.2.cloned.1.call-done = f32[2048,128]{1,0:T(8,128)} async-done(((f32[8192,128]{1,0:T(8,128)}), f32[2048,128]{1,0:T(8,128)}) %reduce-scatter.2.cloned.1.call-update) | async-done | bytes 1048592 | tf_op jit(solution)/shard_map/reduce_scatter | solution.py:109
  (128 shorter events, 24.5 us)
Async XLA Ops:
  6.5 615.4 %reduce-scatter.2.cloned.1.call-start = ((), (), s32[]{:S(2)}) async-start(), calls=%async_computation.1 | async-start | bytes 5242880 | tf_op jit(solution)/shard_map/reduce_scatter | solution.py:109
  6.5 48.7 %collective-permute-start = (bf16[512,32,128]{2,1,0:T(8,128)(2,1)}, bf16[512,32,128]{2,1,0:T(8,128)(2,1)}, u32[]{:S(2)}, u32[]{:S(2)}) collective-permute-start(bf16[512,32,128]{2,1,0:T(8,128)(2,1)} %param.6), channel_id=1, source_target_pairs={{4,0},{8,4},{12,8},{0,12},{5,1},{9,5},{13,9},{1,13},{6,2},{10,6},{... | collective-permute-start | bytes 12582920 | tf_op jit(solution)/shard_map/ppermute | solution.py:14
  55.3 48.2 %collective-permute-start.1 = (bf16[512,32,128]{2,1,0:T(8,128)(2,1)}, bf16[512,32,128]{2,1,0:T(8,128)(2,1)}, u32[]{:S(2)}, u32[]{:S(2)}) collective-permute-start(bf16[512,32,128]{2,1,0:T(8,128)(2,1)} %collective-permute-done), channel_id=1, source_target_pairs={{4,0},{8,4},{12,8},{0,12},{5,1},{9,5},{13,9},{1,13},{6,2},{10,6},{... | collective-permute-start | bytes 12582920 | tf_op jit(solution)/shard_map/ppermute | solution.py:14
  58.1 9.0 %copy-start.4 = (s32[4096]{0:T(1024)S(1)}, s32[4096]{0:T(1024)}, u32[]{:S(2)}) copy-start(s32[4096]{0:T(1024)} %param.9) | copy-start | bytes 49156
  58.1 28.5 %copy-start.2 = (s32[2,4096]{1,0:T(2,128)S(1)}, s32[2,4096]{1,0:T(2,128)}, u32[]{:S(2)}) copy-start(s32[2,4096]{1,0:T(2,128)} %param.8) | copy-start | bytes 98308
  122.4 381.9 %copy-start.3 = (f32[1,4096]{1,0:T(1,128)S(1)}, f32[1,4096]{1,0:T(1,128)}, u32[]{:S(2)}) copy-start(f32[1,4096]{1,0:T(1,128)} %subtract_multiply_fusion) | copy-start | bytes 49156
  122.4 381.9 %copy-start.6 = (s32[128]{0:T(128)S(1)}, s32[128]{0:T(128)}, u32[]{:S(2)}) copy-start(s32[128]{0:T(128)} %and_select_fusion) | copy-start | bytes 1540
  122.4 381.9 %copy-start.7 = (pred[128]{0:T(512)(128)(4,1)S(1)}, pred[128]{0:T(512)(128)(4,1)}, u32[]{:S(2)}) copy-start(pred[128]{0:T(512)(128)(4,1)} %iota_compare_fusion.3) | copy-start | bytes 388
  122.4 381.9 %copy-start.8 = (f32[128]{0:T(128)S(1)}, f32[128]{0:T(128)}, u32[]{:S(2)}) copy-start(f32[128]{0:T(128)} %get-tuple-element.62) | copy-start | bytes 1540
  122.4 381.9 %copy-start.9 = (f32[128]{0:T(128)S(1)}, f32[128]{0:T(128)}, u32[]{:S(2)}) copy-start(f32[128]{0:T(128)} %get-tuple-element.63) | copy-start | bytes 1540
  158.9 2.2 copy-start
  206.6 2.2 copy-start
  254.3 2.2 copy-start
  302.1 2.2 copy-start
  349.8 2.2 copy-start
  397.5 2.2 copy-start
  445.2 2.2 copy-start
  492.9 2.2 copy-start
  504.4 3.8 copy-start.1
  508.1 27.7 %copy-start.5 = (pred[8192]{0:T(1024)(128)(4,1)S(1)}, pred[8192]{0:T(1024)(128)(4,1)}, u32[]{:S(2)}) copy-start(pred[8192]{0:T(1024)(128)(4,1)} %compare_and_fusion.2) | copy-start | bytes 24580
Sparse Core Ops, SparseCore 0:
  543.5 78.4 reduce-scatter.1
where the time goes:
time: 631 us; the launch traced here: 629 us
  local copies, waits for them, and re-layouts  327 us (52%)
  waiting for transfers between devices  141 us (22%)
  other arithmetic  137 us (22%)
  between operations  14.2 us (2%)
    gather x8, local copies, waits for them, and re-layouts, cross_block(): jnp.take(nearby, receiver_ids, axis=0)  118 us
    gather x8, local copies, waits for them, and re-layouts, cross_block(): jnp.take(own_rows, source_ids, axis=0)  90.3 us
    reduce_scatter x1, waiting for transfers between devices, shards(): return lax.psum_scatter(buffer, 'tm', scatter_dimension=0, tiled=True)  78.6 us
    dot_general x8, other arithmetic, pair_spectra(): jnp.einsum('pwf,pwf->pf', source_im, receiver_im, preferred_element_type=...  66.5 us
    ppermute x2, waiting for transfers between devices, from_behind(): return lax.ppermute(block, axis, route)  62.6 us
    while x32, local copies, waits for them, and re-layouts  56.6 us
    gather x1, local copies, waits for them, and re-layouts, shards(): buffer = jnp.take(weighted, slot_pairs, axis=0, mode='fill', fill_value=0.0)  27.7 us
    select_n x8, other arithmetic, cross_block(): jnp.take(own_rows, source_ids, axis=0)  25.9 us
  transfers between devices with their start and end apart: 3, of which 3 were waited for; matrix products, arithmetic and copies ran while one was open for 5% of the time, Pallas kernels for 0%

commit v1 on v0

v1 whole, which is shorter than its diff:
```python
import math

import jax
import jax.numpy as jnp
import numpy as np
from jax import lax
from jax.experimental import pallas as pl
from jax.experimental.pallas import tpu as pltpu
from jax.sharding import PartitionSpec as P

K_SH = 2
GROUP = 16


def from_behind(block, axis, distance):
    devices = range(lax.axis_size(axis))
    route = [((i - distance) % len(devices), i) for i in devices]
    return lax.ppermute(block, axis, route)


def inverse_table(half_bins):
    length = 2 * half_bins
    row_ids = np.arange(length)
    frequency = row_ids % half_bins
    phases = (frequency[:, None] * np.arange(length)[None, :] % length) * (2.0 * math.pi / length)
    weights = np.where(frequency == 0, 1.0, 2.0)[:, None]
    return np.where(
        (row_ids >= half_bins)[:, None], -weights * np.sin(phases), weights * np.cos(phases)
    ).astype(np.float32)


def gather_rows(parts):
    row = lax.broadcasted_iota(jnp.int32, parts[0].shape, 0)
    span = 4
    while span:
        keep = (row // span) % 2 == 0
        half = len(parts) // 2
        parts = [
            jnp.where(keep, parts[k], pltpu.roll(parts[k + half], span, 0))
            + jnp.where(keep, pltpu.roll(parts[k], 8 - span, 0), parts[k + half])
            for k in range(half)
        ]
        span //= 2
    return parts[0]


def sum_tiles(rows):
    total = rows[0:8]
    for start in range(8, rows.shape[0], 8):
        total = total + rows[start : start + 8]
    return total


def cross_rows(sources, receivers, near, turned, total, add):
    npairs = total.shape[0]
    half = total.shape[1] // 2

    def step(group, carry):
        first = pl.multiple_of(group * GROUP, GROUP)
        for offset in range(0, GROUP, 8):
            same, crossed = [], []
            for k in range(8):
                pair = first + offset + k
                source = sources[pair]
                receiver_row = near[receivers[pair]].astype(jnp.float32)
                same.append(sum_tiles(near[source].astype(jnp.float32) * receiver_row))
                crossed.append(sum_tiles(turned[source].astype(jnp.float32) * receiver_row))
            same = gather_rows(same)
            crossed = gather_rows(crossed)
            lane = lax.broadcasted_iota(jnp.int32, same.shape, 1)
            rows = jnp.where(
                lane < half,
                same + pltpu.roll(same, half, 1),
                pltpu.roll(crossed, half, 1) - crossed,
            )
            place = pl.ds(pl.multiple_of(first + offset, 8), 8)
            if add:
                rows = rows + total[place, :]
            total[place, :] = rows
        return carry

    lax.fori_loop(0, npairs // GROUP, step, 0)


def turn_rows(near, turned):
    half = turned.shape[2] // 2

    def step(channel, carry):
        turned[channel] = pltpu.roll(near[channel].astype(jnp.float32), half, 1).astype(
            jnp.bfloat16
        )
        return carry

    lax.fori_loop(0, turned.shape[0], step, 0, unroll=8)


def cross_kernel(sources, receivers, own, ahead, second, total, near, turned, sems):
    rows = own.shape[0]
    copies = [
        pltpu.make_async_copy(block, near.at[pl.ds(k * rows, rows)], sems.at[k])
        for k, block in enumerate((own, ahead, second))
    ]
    for copy in copies:
        copy.start()
    copies[0].wait()
    turn_rows(near, turned)
    for copy in copies[1:]:
        copy.wait()
    cross_rows(sources, receivers, near, turned, total, False)


def stack_kernel(owners, tapering, sums, table, out, rows):
    me = lax.axis_index("tm")
    npairs = sums.shape[0]
    capacity, length = out.shape
    rows[...] = jnp.zeros_like(rows)

    def step(group, count):
        for k in range(8):
            pair = group * 8 + k
            rows[pl.ds(count, 1), :] = sums[pl.ds(pair, 1), :] * tapering[pair]
            count = count + (owners[pair] == me).astype(jnp.int32)
        return count

    count = lax.fori_loop(0, npairs // 8, step, jnp.int32(0))
    rows[pl.ds(count, 1), :] = jnp.zeros((1, length), jnp.float32)
    out[...] = jnp.dot(
        rows[0:capacity, :],
        table[...],
        precision=lax.Precision.HIGHEST,
        preferred_element_type=jnp.float32,
    )


def shards(spectra, band_width, pair_list, owner_ids):
    channel_rows, window_rows, length = spectra.shape
    npairs = pair_list.shape[1]
    tm_size = lax.axis_size("tm")
    capacity = 2 * npairs // tm_size
    windows = window_rows * tm_size
    ahead = from_behind(spectra, "chan", -1)
    second = from_behind(spectra, "chan", -2)
    sources = pair_list[0]
    offsets = pair_list[1]
    receivers = sources + offsets
    smem = pl.BlockSpec(memory_space=pltpu.SMEM)
    vmem = pl.BlockSpec(memory_space=pltpu.VMEM)
    hbm = pl.BlockSpec(memory_space=pl.ANY)
    total = pl.pallas_call(
        cross_kernel,
        out_shape=jax.ShapeDtypeStruct((npairs, length), jnp.float32),
        in_specs=[smem, smem, hbm, hbm, hbm],
        out_specs=vmem,
        scratch_shapes=[
            pltpu.VMEM(((K_SH + 1) * channel_rows, window_rows, length), jnp.bfloat16),
            pltpu.VMEM((channel_rows, window_rows, length), jnp.bfloat16),
            pltpu.SemaphoreType.DMA((3,)),
        ],
        compiler_params=pltpu.CompilerParams(vmem_limit_bytes=40 * 2**20),
        cost_estimate=pl.CostEstimate(
            flops=8 * npairs * window_rows * length, bytes_accessed=14 * 2**20, transcendentals=0
        ),
    )(sources, receivers, spectra, ahead, second)
    total = lax.psum(total, "tm")
    tapering = (1.0 - offsets.astype(jnp.float32) / band_width[0].astype(jnp.float32)) / windows
    return pl.pallas_call(
        stack_kernel,
        out_shape=jax.ShapeDtypeStruct((capacity, length), jnp.float32),
        in_specs=[smem, smem, vmem, vmem],
        out_specs=vmem,
        scratch_shapes=[pltpu.VMEM((capacity + 8, length), jnp.float32)],
        compiler_params=pltpu.CompilerParams(vmem_limit_bytes=32 * 2**20),
        cost_estimate=pl.CostEstimate(
            flops=12 * capacity * length * length, bytes_accessed=3 * 2**20, transcendentals=0
        ),
    )(owner_ids, tapering, total, jnp.asarray(inverse_table(length // 2)))


def solution(mesh):
    return jax.shard_map(
        shards,
        mesh=mesh,
        in_specs=(
            P(("grp", "chan"), "tm", None),
            P(("grp", "chan")),
            P(None, ("grp", "chan")),
            P(("grp", "chan")),
        ),
        out_specs=P(("grp", "chan", "tm"), None),
        check_vma=False,
    )
```

time: 631 us -> 311 us (0.49)
  local copies, waits for them, and re-layouts: 327 us -> 6.59 us
  other arithmetic: 137 us -> 0.01 us
  waiting for transfers between devices: 141 us -> 223 us
  Pallas kernels: 0 us -> 63.9 us
    gather x17 -> x0, local copies, waits for them, and re-layouts: 236 us -> none  [the longest x8 118 us: cross_block(): jnp.take(nearby, receiver_ids, axis=0)]
    psum x0 -> x1, waiting for transfers between devices: none -> 87.4 us  [shards(): total = lax.psum(total, 'tm')]
    reduce_scatter x1 -> x0, waiting for transfers between devices: 78.6 us -> none  [shards(): return lax.psum_scatter(buffer, 'tm', scatter_dimension=0, tiled=True)]
    ppermute x2, waiting for transfers between devices: 62.6 us -> 136 us  [from_behind(): return lax.ppermute(block, axis, route)]
    dot_general x8 -> x0, other arithmetic: 66.5 us -> none  [pair_spectra(): jnp.einsum('pwf,pwf->pf', source_im, receiver_im, preferred_element_type=...]
    pallas_call x0 -> x2, Pallas kernels: none -> 63.9 us  [the longest x1 49.7 us: shards(): pl.pallas_call(cross_kernel, out_shape=jax.ShapeDtypeStruct((npairs, leng...]
    while x32 -> x0, local copies, waits for them, and re-layouts: 56.6 us -> none
    select_n x28 -> x0, other arithmetic: 50.2 us -> none  [the longest x8 25.9 us: cross_block(): jnp.take(own_rows, source_ids, axis=0)]
  transfers between devices with their start and end apart: 3 -> 3, of which waited for: 3 -> 3; matrix products, arithmetic and copies ran while one was open for 5% -> 0% of each run, Pallas kernels for 0% -> 0%
where the time goes in v1:
time: 311 us; the launch traced here: 310 us
  waiting for transfers between devices  223 us (72%)
  Pallas kernels  63.9 us (21%)
  between operations  14.1 us (5%)
  local copies, waits for them, and re-layouts  6.59 us (2%)
    ppermute x2, waiting for transfers between devices, from_behind(): return lax.ppermute(block, axis, route)  136 us
    psum x1, waiting for transfers between devices, shards(): total = lax.psum(total, 'tm')  87.4 us
    pallas_call x1, Pallas kernels, shards(): pl.pallas_call(cross_kernel, out_shape=jax.ShapeDtypeStruct((npairs, leng...  49.7 us
    pallas_call x1, Pallas kernels, shards(): pl.pallas_call(stack_kernel, out_shape=jax.ShapeDtypeStruct((capacity, le...  14.1 us
  transfers between devices with their start and end apart: 3, of which 3 were waited for; matrix products, arithmetic and copies ran while one was open for 0% of the time, Pallas kernels for 0%

profile of v1, /device:TPU:0, one launch (start us, length us, event | category | flops | bytes accessed | tf_op | source)
XLA Modules:
  0.0 310.4 jit_solution(13454725315635536179)
XLA Ops:
  6.5 0.0 all-reduce.2.cloned.1.call-start
  6.5 2.4 collective-permute-start
  8.9 0.6 collective-permute-start.1
  9.5 0.9 fusion
  10.3 0.0 copy-start.3
  10.4 89.7 %collective-permute-done.ahead = bf16[512,32,128]{2,1,0:T(8,128)(2,1)S(1)} collective-permute-done((bf16[512,32,128]{2,1,0:T(8,128)(2,1)}, bf16[512,32,128]{2,1,0:T(8,128)(2,1)S(1)}, u32[]{:S(2)}, u32[]{:S(2)}) %collective-permute-start) | collective-permute-done | bytes 4194336 | tf_op jit(solution)/shard_map/ppermute | solution.py:18
  100.1 45.8 %collective-permute-done.1.second = bf16[512,32,128]{2,1,0:T(8,128)(2,1)S(1)} collective-permute-done((bf16[512,32,128]{2,1,0:T(8,128)(2,1)}, bf16[512,32,128]{2,1,0:T(8,128)(2,1)S(1)}, u32[]{:S(2)}, u32[]{:S(2)}) %collective-permute-start.1) | collective-permute-done | bytes 4194336 | tf_op jit(solution)/shard_map/ppermute | solution.py:18
  145.9 0.0 copy-start.4
  145.9 1.9 copy-done.4
  147.8 0.0 copy-start
  147.8 2.2 copy-done
  150.0 0.0 copy-start.2
  150.0 49.7 %shard_map.55 = f32[4096,128]{1,0:T(8,128)} custom-call(s32[4096]{0:T(1024)S(1)} %bitcast.4, s32[4096]{0:T(1024)S(1)} %add.5.receivers, bf16[512,32,128]{2,1,0:T(8,128)(2,1)S(1)} %copy-done, bf16[512,32,128]{2,1,0:T(8,128)(2,1)S(1)} %collective-permute-done.ahead, bf16[512,32,128]{2,1,0:T(8,128)(2,1)} %copy-done.4), custom_call_target="tpu_custom_call" | custom-call | flops 134217728 | bytes 14680064 | tf_op jit(solution)/shard_map/pallas_call | solution.py:149
  199.8 0.0 all-reduce.2.cloned.1.call-update
  200.4 87.4 %all-reduce.2.cloned.1.call-done.sums = f32[4096,128]{1,0:T(8,128)} async-done(((f32[4096,128]{1,0:T(8,128)}), f32[4096,128]{1,0:T(8,128)}) %all-reduce.2.cloned.1.call-update) | async-done | bytes 2097168 | tf_op jit(solution)/shard_map/psum | solution.py:164
  287.8 0.0 copy-done.3
  287.8 0.0 copy-done.2
  287.8 0.0 copy-start.1
  287.8 1.6 copy-done.1
  289.4 14.1 %shard_map.56 = f32[2048,128]{1,0:T(8,128)} custom-call(s32[4096]{0:T(1024)S(1)} %copy-done.3, f32[4096]{0:T(1024)S(1)} %subtract_multiply_fusion.tapering, f32[4096,128]{1,0:T(8,128)S(1)} %copy-done.1, f32[128,128]{1,0:T(8,128)S(1)} %copy-done.2), custom_call_target="tpu_custom_call" | custom-call | flops 402653184 | bytes 3145728 | tf_op jit(solution)/shard_map/pallas_call | solution.py:166
  (2 shorter events, 0.0 us)
Async XLA Ops:
  6.5 281.3 %all-reduce.2.cloned.1.call-start = ((), (), s32[]{:S(2)}) async-start(), calls=%async_computation | async-start | bytes 4194304 | tf_op jit(solution)/shard_map/psum | solution.py:164
  6.5 93.6 %collective-permute-start = (bf16[512,32,128]{2,1,0:T(8,128)(2,1)}, bf16[512,32,128]{2,1,0:T(8,128)(2,1)S(1)}, u32[]{:S(2)}, u32[]{:S(2)}) collective-permute-start(bf16[512,32,128]{2,1,0:T(8,128)(2,1)} %own.1), channel_id=1, source_target_pairs={{4,0},{8,4},{12,8},{0,12},{5,1},{9,5},{13,9},{1,13},{6,2},{10,6},{... | collective-permute-start | bytes 12582920 | tf_op jit(solution)/shard_map/ppermute | solution.py:18
  8.9 137.0 %collective-permute-start.1 = (bf16[512,32,128]{2,1,0:T(8,128)(2,1)}, bf16[512,32,128]{2,1,0:T(8,128)(2,1)S(1)}, u32[]{:S(2)}, u32[]{:S(2)}) collective-permute-start(bf16[512,32,128]{2,1,0:T(8,128)(2,1)} %own.1), channel_id=1, source_target_pairs={{8,0},{12,4},{0,8},{4,12},{9,1},{13,5},{1,9},{5,13},{10,2},{14,6},... | collective-permute-start | bytes 12582920 | tf_op jit(solution)/shard_map/ppermute | solution.py:18
  10.3 277.5 %copy-start.3 = (s32[4096]{0:T(1024)S(1)}, s32[4096]{0:T(1024)}, u32[]{:S(2)}) copy-start(s32[4096]{0:T(1024)} %owners.1) | copy-start | bytes 49156
  145.9 1.9 copy-start.4
  147.8 2.2 copy-start
  150.0 137.8 %copy-start.2 = (f32[128,128]{1,0:T(8,128)S(1)}, f32[128,128]{1,0:T(8,128)}, u32[]{:S(2)}) copy-start(f32[128,128]{1,0:T(8,128)} %constant.7.clone.table) | copy-start | bytes 196612
  287.8 1.6 copy-start.1
Sparse Core Ops, SparseCore 0:
  199.9 87.8 all-reduce.1

commit v2 on v1

--- a/solution.py
+++ b/solution.py
@@ -1,3 +1,4 @@
+import functools
 import math
 
 import jax
@@ -10,12 +11,11 @@
 
 K_SH = 2
 GROUP = 16
-
-
-def from_behind(block, axis, distance):
-    devices = range(lax.axis_size(axis))
-    route = [((i - distance) % len(devices), i) for i in devices]
-    return lax.ppermute(block, axis, route)
+CHUNK = 16
+PIECES = 4
+DEPTH = 3
+FLOWS = 16
+MESH = pl.DeviceIdType.MESH
 
 
 def inverse_table(half_bins):
@@ -51,12 +51,11 @@
     return total
 
 
-def cross_rows(sources, receivers, near, turned, total, add):
-    npairs = total.shape[0]
+def cross_rows(sources, receivers, near, turned, total, start, count, add):
     half = total.shape[1] // 2
 
     def step(group, carry):
-        first = pl.multiple_of(group * GROUP, GROUP)
+        first = pl.multiple_of(start + group * GROUP, GROUP)
         for offset in range(0, GROUP, 8):
             same, crossed = [], []
             for k in range(8):
@@ -79,7 +78,7 @@
             total[place, :] = rows
         return carry
 
-    lax.fori_loop(0, npairs // GROUP, step, 0)
+    lax.fori_loop(0, count // GROUP, step, 0)
 
 
 def turn_rows(near, turned):
@@ -94,19 +93,212 @@
     lax.fori_loop(0, turned.shape[0], step, 0, unroll=8)
 
 
-def cross_kernel(sources, receivers, own, ahead, second, total, near, turned, sems):
+def exchange_kernel(
+    nchan, ntm, sources, receivers, own, total, *scratch
+):
+    chunks = own.shape[1] // CHUNK
+    near = scratch[:chunks]
+    (
+        turned, mine, from_left, to_right, from_right, to_left,
+        own_sems, far_send, far_recv, pass_send, pass_recv,
+        right_send, right_recv, left_send, left_recv,
+    ) = scratch[chunks:]
     rows = own.shape[0]
-    copies = [
-        pltpu.make_async_copy(block, near.at[pl.ds(k * rows, rows)], sems.at[k])
-        for k, block in enumerate((own, ahead, second))
-    ]
-    for copy in copies:
+    piece_rows = rows // PIECES
+    chan = lax.axis_index("chan")
+    me = lax.axis_index("tm")
+    core = lax.rem(chan, 2)
+    partner = chan + 1 - 2 * core
+    behind = lax.rem(chan + nchan - 2, nchan)
+    beyond = lax.rem(chan + 2, nchan)
+    last = ntm - 1
+
+    barrier = pltpu.get_barrier_semaphore()
+    peers = (behind, partner) if nchan == 4 else (behind, beyond, partner)
+    for device in peers:
+        pl.semaphore_signal(barrier, inc=1, device_id={"chan": device}, device_id_type=MESH)
+
+    @pl.when(me > 0)
+    def _():
+        pl.semaphore_signal(barrier, inc=1, device_id={"tm": me - 1}, device_id_type=MESH)
+
+    @pl.when(me < last)
+    def _():
+        pl.semaphore_signal(barrier, inc=1, device_id={"tm": me + 1}, device_id_type=MESH)
+
+    own_copies = []
+    for chunk in range(chunks):
+        copy = pltpu.make_async_copy(
+            own.at[:, pl.ds(chunk * CHUNK, CHUNK), :],
+            near[chunk].at[pl.ds(0, rows)],
+            own_sems.at[chunk],
+        )
+        own_copies.append(copy)
+    own_copies[0].start()
+
+    pl.semaphore_wait(
+        barrier, len(peers) + (me > 0).astype(jnp.int32) + (me < last).astype(jnp.int32)
+    )
+
+    def own_piece(number):
+        chunk, piece = divmod(number, PIECES)
+        return own.at[pl.ds(piece * piece_rows, piece_rows), pl.ds(chunk * CHUNK, CHUNK), :]
+
+    def near_piece(number, block):
+        chunk, piece = divmod(number, PIECES)
+        return near[chunk].at[pl.ds(block * rows + piece * piece_rows, piece_rows)]
+
+    def far(number):
+        return pltpu.make_async_remote_copy(
+            src_ref=own_piece(number),
+            dst_ref=near_piece(number, 2),
+            send_sem=far_send.at[number],
+            recv_sem=far_recv.at[number],
+            device_id={"chan": behind},
+            device_id_type=MESH,
+        )
+
+    def handed(number, source):
+        return pltpu.make_async_remote_copy(
+            src_ref=source,
+            dst_ref=near_piece(number, 1),
+            send_sem=pass_send.at[number],
+            recv_sem=pass_recv.at[number],
+            device_id={"chan": partner},
+            device_id_type=MESH,
+        )
+
+    count = chunks * PIECES
+    for number in range(min(DEPTH, count)):
+        far(number).start()
+
+    for copy in own_copies[1:]:
         copy.start()
-    copies[0].wait()
-    turn_rows(near, turned)
-    for copy in copies[1:]:
-        copy.wait()
-    cross_rows(sources, receivers, near, turned, total, False)
+
+    @pl.when(core == 1)
+    def _():
+        for number in range(count):
+            handed(number, own_piece(number)).start()
+
+    def arrive(number):
+        far(number).wait_recv()
+        if number + DEPTH < count:
+            far(number + DEPTH).start()
+
+        @pl.when(core == 0)
+        def _():
+            handed(number, near_piece(number, 2)).start()
+
+    group_rows = mine.shape[0] // FLOWS
+    for chunk in range(chunks):
+        own_copies[chunk].wait()
+        turn_rows(near[chunk], turned)
+        for piece in range(PIECES):
+            arrive(chunk * PIECES + piece)
+        for piece in range(PIECES):
+            handed(chunk * PIECES + piece, own_piece(chunk * PIECES + piece)).wait_recv()
+        if chunk < chunks - 1:
+            cross_rows(
+                sources, receivers, near[chunk], turned, mine, 0, mine.shape[0], chunk > 0
+            )
+
+    def flow(source, target, send_sem, recv_sem, group, device):
+        place = pl.ds(pl.multiple_of(group * group_rows, group_rows), group_rows)
+        return pltpu.make_async_remote_copy(
+            src_ref=source.at[place],
+            dst_ref=target.at[place],
+            send_sem=send_sem.at[group],
+            recv_sem=recv_sem.at[group],
+            device_id={"tm": device},
+            device_id_type=MESH,
+        )
+
+    def rightward(group):
+        return flow(to_right, from_left, right_send, right_recv, group, lax.rem(me + 1, ntm))
+
+    def leftward(group):
+        return flow(to_left, from_right, left_send, left_recv, group, lax.rem(me + last, ntm))
+
+    def place_of(group):
+        return pl.ds(pl.multiple_of(group * group_rows, group_rows), group_rows)
+
+    def stage(step, carry):
+        @pl.when(step < FLOWS)
+        def _():
+            cross_rows(
+                sources, receivers, near[chunks - 1], turned, mine,
+                step * group_rows, group_rows, chunks > 1,
+            )
+
+        right_group = step - me
+
+        @pl.when((right_group >= 0) & (right_group < FLOWS) & (me < last))
+        def _():
+            place = place_of(right_group)
+
+            @pl.when(me > 0)
+            def _():
+                rightward(right_group).wait_recv()
+                to_right[place, :] = mine[place, :] + from_left[place, :]
+
+            @pl.when(me == 0)
+            def _():
+                to_right[place, :] = mine[place, :]
+
+            rightward(right_group).start()
+
+        left_group = step - (last - me)
+
+        @pl.when((left_group >= 0) & (left_group < FLOWS) & (me > 0))
+        def _():
+            place = place_of(left_group)
+
+            @pl.when(me < last)
+            def _():
+                leftward(left_group).wait_recv()
+                to_left[place, :] = mine[place, :] + from_right[place, :]
+
+            @pl.when(me == last)
+            def _():
+                to_left[place, :] = mine[place, :]
+
+            leftward(left_group).start()
+
+        return carry
+
+    lax.fori_loop(0, FLOWS + ntm - 1, stage, 0)
+
+    def finish(group, carry):
+        place = place_of(group)
+
+        @pl.when(me == 0)
+        def _():
+            leftward(group).wait_recv()
+            total[place, :] = mine[place, :] + from_right[place, :]
+
+        @pl.when(me == last)
+        def _():
+            rightward(group).wait_recv()
+            total[place, :] = mine[place, :] + from_left[place, :]
+
+        @pl.when((me > 0) & (me < last))
+        def _():
+            total[place, :] = to_right[place, :] + from_right[place, :]
+
+        @pl.when(me < last)
+        def _():
+            rightward(group).wait_send()
+
+        @pl.when(me > 0)
+        def _():
+            leftward(group).wait_send()
+
+        return carry
+
+    lax.fori_loop(0, FLOWS, finish, 0)
+    for number in range(count):
+        far(number).wait_send()
+        handed(number, own_piece(number)).wait_send()
 
 
 def stack_kernel(owners, tapering, sums, table, out, rows):
@@ -138,30 +330,32 @@
     tm_size = lax.axis_size("tm")
     capacity = 2 * npairs // tm_size
     windows = window_rows * tm_size
-    ahead = from_behind(spectra, "chan", -1)
-    second = from_behind(spectra, "chan", -2)
     sources = pair_list[0]
     offsets = pair_list[1]
     receivers = sources + offsets
     smem = pl.BlockSpec(memory_space=pltpu.SMEM)
     vmem = pl.BlockSpec(memory_space=pltpu.VMEM)
     hbm = pl.BlockSpec(memory_space=pl.ANY)
+    chunks = window_rows // CHUNK
+    flow_buffer = pltpu.VMEM((npairs, length), jnp.float32)
     total = pl.pallas_call(
-        cross_kernel,
+        functools.partial(exchange_kernel, lax.axis_size("chan"), tm_size),
         out_shape=jax.ShapeDtypeStruct((npairs, length), jnp.float32),
-        in_specs=[smem, smem, hbm, hbm, hbm],
+        in_specs=[smem, smem, hbm],
         out_specs=vmem,
-        scratch_shapes=[
-            pltpu.VMEM(((K_SH + 1) * channel_rows, window_rows, length), jnp.bfloat16),
-            pltpu.VMEM((channel_rows, window_rows, length), jnp.bfloat16),
-            pltpu.SemaphoreType.DMA((3,)),
-        ],
-        compiler_params=pltpu.CompilerParams(vmem_limit_bytes=40 * 2**20),
+        scratch_shapes=[pltpu.VMEM(((K_SH + 1) * channel_rows, CHUNK, length), jnp.bfloat16)] * chunks
+        + [pltpu.VMEM((channel_rows, CHUNK, length), jnp.bfloat16)]
+        + [flow_buffer] * 5
+        + [pltpu.SemaphoreType.DMA((chunks,))]
+        + [pltpu.SemaphoreType.DMA((chunks * PIECES,))] * 4
+        + [pltpu.SemaphoreType.DMA((FLOWS,))] * 4,
+        compiler_params=pltpu.CompilerParams(
+            vmem_limit_bytes=48 * 2**20, collective_id=0, has_side_effects=True
+        ),
         cost_estimate=pl.CostEstimate(
             flops=8 * npairs * window_rows * length, bytes_accessed=14 * 2**20, transcendentals=0
         ),
-    )(sources, receivers, spectra, ahead, second)
-    total = lax.psum(total, "tm")
+    )(sources, receivers, spectra)
     tapering = (1.0 - offsets.astype(jnp.float32) / band_width[0].astype(jnp.float32)) / windows
     return pl.pallas_call(
         stack_kernel,

time: 311 us -> 193 us (0.62)
  waiting for transfers between devices: 223 us -> 0 us
  Pallas kernels: 63.9 us -> 191 us
  between operations: 14.1 us -> 0.73 us
  local copies, waits for them, and re-layouts: 6.59 us -> 0.87 us
    ppermute x2 -> x0, waiting for transfers between devices: 136 us -> none  [from_behind(): return lax.ppermute(block, axis, route)]
    pallas_call x1, Pallas kernels: 49.7 us -> 177 us  [shards(): pl.pallas_call(functools.partial(exchange_kernel, lax.axis_size('chan'),...]
    psum x1 -> x0, waiting for transfers between devices: 87.4 us -> none  [shards(): total = lax.psum(total, 'tm')]
    unnamed x10 -> x4, local copies, waits for them, and re-layouts: 5.72 us -> 0.01 us
  transfers between devices with their start and end apart: 3 -> 0, of which waited for: 3 -> 0; matrix products, arithmetic and copies ran while one was open for 0% -> 0% of each run, Pallas kernels for 0% -> 0%
where the time goes in v2:
time: 193 us
  Pallas kernels  191 us (99%)
    pallas_call x1, Pallas kernels, shards(): pl.pallas_call(functools.partial(exchange_kernel, lax.axis_size('chan'),...  177 us
    pallas_call x1, Pallas kernels, shards(): pl.pallas_call(stack_kernel, out_shape=jax.ShapeDtypeStruct((capacity, le...  14.1 us

profile of v2, /device:TPU:0, one launch (start us, length us, event | category | flops | bytes accessed | tf_op | source)
XLA Modules:
  0.0 192.9 jit_solution(16712476036411257217)
XLA Ops:
  0.0 0.0 copy-start
  0.0 0.0 copy-start.1
  0.7 0.9 fusion
  1.6 177.2 %shard_map.55.sums = f32[4096,128]{1,0:T(8,128)S(1)} custom-call(s32[4096]{0:T(1024)S(1)} %bitcast.4, s32[4096]{0:T(1024)S(1)} %add.3.receivers, bf16[512,32,128]{2,1,0:T(8,128)(2,1)} %own.1), custom_call_target="tpu_custom_call" | custom-call | flops 134217728 | bytes 14680064 | tf_op jit(solution)/shard_map/pallas_call | solution.py:341
  178.8 0.0 copy-done
  178.8 0.0 copy-done.1
  178.8 14.1 %shard_map.56 = f32[2048,128]{1,0:T(8,128)} custom-call(s32[4096]{0:T(1024)S(1)} %copy-done.1, f32[4096]{0:T(1024)S(1)} %subtract_multiply_fusion.tapering, f32[4096,128]{1,0:T(8,128)S(1)} %shard_map.55.sums, f32[128,128]{1,0:T(8,128)S(1)} %copy-done), custom_call_target="tpu_custom_call" | custom-call | flops 402653184 | bytes 3145728 | tf_op jit(solution)/shard_map/pallas_call | solution.py:360
  (2 shorter events, 0.0 us)
Async XLA Ops:
  0.0 178.8 %copy-start = (f32[128,128]{1,0:T(8,128)S(1)}, f32[128,128]{1,0:T(8,128)}, u32[]{:S(2)}) copy-start(f32[128,128]{1,0:T(8,128)} %constant.7.clone.table) | copy-start | bytes 196612
  0.0 178.8 %copy-start.1 = (s32[4096]{0:T(1024)S(1)}, s32[4096]{0:T(1024)}, u32[]{:S(2)}) copy-start(s32[4096]{0:T(1024)} %owners.1) | copy-start | bytes 49156

commit v3 on v2

--- a/solution.py
+++ b/solution.py
@@ -13,8 +13,9 @@
 GROUP = 16
 CHUNK = 16
 PIECES = 4
-DEPTH = 3
-FLOWS = 16
+DEPTH = 4
+FLOWS = 32
+LAG = 2
 MESH = pl.DeviceIdType.MESH
 
 
@@ -230,7 +231,7 @@
                 step * group_rows, group_rows, chunks > 1,
             )
 
-        right_group = step - me
+        right_group = step - LAG * me
 
         @pl.when((right_group >= 0) & (right_group < FLOWS) & (me < last))
         def _():
@@ -247,7 +248,7 @@
 
             rightward(right_group).start()
 
-        left_group = step - (last - me)
+        left_group = step - LAG * (last - me)
 
         @pl.when((left_group >= 0) & (left_group < FLOWS) & (me > 0))
         def _():
@@ -266,7 +267,7 @@
 
         return carry
 
-    lax.fori_loop(0, FLOWS + ntm - 1, stage, 0)
+    lax.fori_loop(0, FLOWS + LAG * last, stage, 0)
 
     def finish(group, carry):
         place = place_of(group)
@@ -308,13 +309,13 @@
     rows[...] = jnp.zeros_like(rows)
 
     def step(group, count):
-        for k in range(8):
-            pair = group * 8 + k
+        for k in range(32):
+            pair = group * 32 + k
             rows[pl.ds(count, 1), :] = sums[pl.ds(pair, 1), :] * tapering[pair]
             count = count + (owners[pair] == me).astype(jnp.int32)
         return count
 
-    count = lax.fori_loop(0, npairs // 8, step, jnp.int32(0))
+    count = lax.fori_loop(0, npairs // 32, step, jnp.int32(0))
     rows[pl.ds(count, 1), :] = jnp.zeros((1, length), jnp.float32)
     out[...] = jnp.dot(
         rows[0:capacity, :],

time: 193 us -> 178 us (0.922)
  Pallas kernels: 191 us -> 176 us
    pallas_call x1, Pallas kernels: 177 us -> 161 us  [shards(): pl.pallas_call(functools.partial(exchange_kernel, lax.axis_size('chan'),...]
where the time goes in v3:
time: 178 us
  Pallas kernels  176 us (99%)
    pallas_call x1, Pallas kernels, shards(): pl.pallas_call(functools.partial(exchange_kernel, lax.axis_size('chan'),...  161 us
    pallas_call x1, Pallas kernels, shards(): pl.pallas_call(stack_kernel, out_shape=jax.ShapeDtypeStruct((capacity, le...  15.5 us

profile of v3, /device:TPU:0, one launch (start us, length us, event | category | flops | bytes accessed | tf_op | source)
XLA Modules:
  0.0 177.8 jit_solution(13693477132569837496)
XLA Ops:
  0.0 0.0 copy-start
  0.0 0.0 copy-start.1
  0.7 0.9 fusion
  1.6 160.7 %shard_map.55.sums = f32[4096,128]{1,0:T(8,128)S(1)} custom-call(s32[4096]{0:T(1024)S(1)} %bitcast.4, s32[4096]{0:T(1024)S(1)} %add.3.receivers, bf16[512,32,128]{2,1,0:T(8,128)(2,1)} %own.1), custom_call_target="tpu_custom_call" | custom-call | flops 134217728 | bytes 14680064 | tf_op jit(solution)/shard_map/pallas_call | solution.py:342
  162.3 0.0 copy-done
  162.3 0.0 copy-done.1
  162.3 15.5 %shard_map.56 = f32[2048,128]{1,0:T(8,128)} custom-call(s32[4096]{0:T(1024)S(1)} %copy-done.1, f32[4096]{0:T(1024)S(1)} %subtract_multiply_fusion.tapering, f32[4096,128]{1,0:T(8,128)S(1)} %shard_map.55.sums, f32[128,128]{1,0:T(8,128)S(1)} %copy-done), custom_call_target="tpu_custom_call" | custom-call | flops 402653184 | bytes 3145728 | tf_op jit(solution)/shard_map/pallas_call | solution.py:361
  (2 shorter events, 0.0 us)
Async XLA Ops:
  0.0 162.3 %copy-start = (f32[128,128]{1,0:T(8,128)S(1)}, f32[128,128]{1,0:T(8,128)}, u32[]{:S(2)}) copy-start(f32[128,128]{1,0:T(8,128)} %constant.7.clone.table) | copy-start | bytes 196612
  0.0 162.3 %copy-start.1 = (s32[4096]{0:T(1024)S(1)}, s32[4096]{0:T(1024)}, u32[]{:S(2)}) copy-start(s32[4096]{0:T(1024)} %owners.1) | copy-start | bytes 49156

commit v4 on v3

--- a/solution.py
+++ b/solution.py
@@ -12,8 +12,8 @@
 K_SH = 2
 GROUP = 16
 CHUNK = 16
-PIECES = 4
-DEPTH = 4
+PIECES = 8
+DEPTH = 8
 FLOWS = 32
 LAG = 2
 MESH = pl.DeviceIdType.MESH
@@ -95,7 +95,7 @@
 
 
 def exchange_kernel(
-    nchan, ntm, sources, receivers, own, total, *scratch
+    nchan, ntm, sources, receivers, owners, tapering, own, total, slots, *scratch
 ):
     chunks = own.shape[1] // CHUNK
     near = scratch[:chunks]
@@ -191,9 +191,21 @@
             handed(number, near_piece(number, 2)).start()
 
     group_rows = mine.shape[0] // FLOWS
+
+    def count_slots(group, held):
+        for k in range(16):
+            pair = group * 16 + k
+            slots[pair] = held
+            held = held + (owners[pair] == me).astype(jnp.int32)
+        return held
+
     for chunk in range(chunks):
         own_copies[chunk].wait()
         turn_rows(near[chunk], turned)
+        if chunk == 0:
+            slots[mine.shape[0]] = lax.fori_loop(
+                0, mine.shape[0] // 16, count_slots, jnp.int32(0)
+            )
         for piece in range(PIECES):
             arrive(chunk * PIECES + piece)
         for piece in range(PIECES):
@@ -271,20 +283,23 @@
 
     def finish(group, carry):
         place = place_of(group)
+        taper = jnp.transpose(
+            jnp.broadcast_to(tapering[pl.ds(group, 1), :], (total.shape[1], group_rows))
+        )
 
         @pl.when(me == 0)
         def _():
             leftward(group).wait_recv()
-            total[place, :] = mine[place, :] + from_right[place, :]
+            total[place, :] = (mine[place, :] + from_right[place, :]) * taper
 
         @pl.when(me == last)
         def _():
             rightward(group).wait_recv()
-            total[place, :] = mine[place, :] + from_left[place, :]
+            total[place, :] = (mine[place, :] + from_left[place, :]) * taper
 
         @pl.when((me > 0) & (me < last))
         def _():
-            total[place, :] = to_right[place, :] + from_right[place, :]
+            total[place, :] = (to_right[place, :] + from_right[place, :]) * taper
 
         @pl.when(me < last)
         def _():
@@ -302,21 +317,21 @@
         handed(number, own_piece(number)).wait_send()
 
 
-def stack_kernel(owners, tapering, sums, table, out, rows):
-    me = lax.axis_index("tm")
+def stack_kernel(slots, sums, table, out, rows):
     npairs = sums.shape[0]
     capacity, length = out.shape
     rows[...] = jnp.zeros_like(rows)
 
-    def step(group, count):
-        for k in range(32):
-            pair = group * 32 + k
-            rows[pl.ds(count, 1), :] = sums[pl.ds(pair, 1), :] * tapering[pair]
-            count = count + (owners[pair] == me).astype(jnp.int32)
-        return count
-
-    count = lax.fori_loop(0, npairs // 32, step, jnp.int32(0))
-    rows[pl.ds(count, 1), :] = jnp.zeros((1, length), jnp.float32)
+    def step(group, carry):
+        first = pl.multiple_of(group * 32, 32)
+        for k in range(0, 32, 8):
+            tile = sums[pl.ds(pl.multiple_of(first + k, 8), 8), :]
+            for j in range(8):
+                rows[pl.ds(slots[first + k + j], 1), :] = tile[j : j + 1]
+        return carry
+
+    lax.fori_loop(0, npairs // 32, step, 0)
+    rows[pl.ds(slots[npairs], 1), :] = jnp.zeros((1, length), jnp.float32)
     out[...] = jnp.dot(
         rows[0:capacity, :],
         table[...],
@@ -337,13 +352,18 @@
     smem = pl.BlockSpec(memory_space=pltpu.SMEM)
     vmem = pl.BlockSpec(memory_space=pltpu.VMEM)
     hbm = pl.BlockSpec(memory_space=pl.ANY)
+    tapering = (1.0 - offsets.astype(jnp.float32) / band_width[0].astype(jnp.float32)) / windows
+    tapering = tapering.reshape(FLOWS, npairs // FLOWS)
     chunks = window_rows // CHUNK
     flow_buffer = pltpu.VMEM((npairs, length), jnp.float32)
-    total = pl.pallas_call(
+    total, slots = pl.pallas_call(
         functools.partial(exchange_kernel, lax.axis_size("chan"), tm_size),
-        out_shape=jax.ShapeDtypeStruct((npairs, length), jnp.float32),
-        in_specs=[smem, smem, hbm],
-        out_specs=vmem,
+        out_shape=(
+            jax.ShapeDtypeStruct((npairs, length), jnp.float32),
+            jax.ShapeDtypeStruct((npairs + 1,), jnp.int32),
+        ),
+        in_specs=[smem, smem, smem, vmem, hbm],
+        out_specs=(vmem, smem),
         scratch_shapes=[pltpu.VMEM(((K_SH + 1) * channel_rows, CHUNK, length), jnp.bfloat16)] * chunks
         + [pltpu.VMEM((channel_rows, CHUNK, length), jnp.bfloat16)]
         + [flow_buffer] * 5
@@ -356,19 +376,18 @@
         cost_estimate=pl.CostEstimate(
             flops=8 * npairs * window_rows * length, bytes_accessed=14 * 2**20, transcendentals=0
         ),
-    )(sources, receivers, spectra)
-    tapering = (1.0 - offsets.astype(jnp.float32) / band_width[0].astype(jnp.float32)) / windows
+    )(sources, receivers, owner_ids, tapering, spectra)
     return pl.pallas_call(
         stack_kernel,
         out_shape=jax.ShapeDtypeStruct((capacity, length), jnp.float32),
-        in_specs=[smem, smem, vmem, vmem],
+        in_specs=[smem, vmem, vmem],
         out_specs=vmem,
         scratch_shapes=[pltpu.VMEM((capacity + 8, length), jnp.float32)],
         compiler_params=pltpu.CompilerParams(vmem_limit_bytes=32 * 2**20),
         cost_estimate=pl.CostEstimate(
             flops=12 * capacity * length * length, bytes_accessed=3 * 2**20, transcendentals=0
         ),
-    )(owner_ids, tapering, total, jnp.asarray(inverse_table(length // 2)))
+    )(slots, total, jnp.asarray(inverse_table(length // 2)))
 
 
 def solution(mesh):

time: 178 us -> 172 us (0.966)
  Pallas kernels: 176 us -> 169 us
    pallas_call x1, Pallas kernels: 15.5 us -> 6.66 us  [shards(): pl.pallas_call(stack_kernel, out_shape=jax.ShapeDtypeStruct((capacity, le...]
where the time goes in v4:
time: 172 us
  Pallas kernels  169 us (98%)
    pallas_call x1, Pallas kernels, shards(): pl.pallas_call(functools.partial(exchange_kernel, lax.axis_size('chan'),...  162 us
    pallas_call x1, Pallas kernels, shards(): pl.pallas_call(stack_kernel, out_shape=jax.ShapeDtypeStruct((capacity, le...  6.66 us

profile of v4, /device:TPU:0, one launch (start us, length us, event | category | flops | bytes accessed | tf_op | source)
XLA Modules:
  0.0 171.7 jit_solution(18078261029703427982)
XLA Ops:
  0.0 0.0 copy-start
  0.7 0.8 subtract_multiply_fusion
  1.5 0.9 fusion
  2.4 0.0 copy-start.1
  2.4 0.7 copy-done.1
  3.1 161.9 %shard_map.55 = (f32[4096,128]{1,0:T(8,128)S(1)}, s32[4097]{0:T(1024)S(1)}) custom-call(s32[4096]{0:T(1024)S(1)} %bitcast.5, s32[4096]{0:T(1024)S(1)} %add.3.receivers, s32[4096]{0:T(1024)S(1)} %copy-done.1, f32[32,128]{1,0:T(8,128)S(1)} %bitcast.6, bf16[512,32,128]{2,1,0:T(8,128)(2,1)} %own.1), custom_call_target="tpu_custom_call" | custom-call | flops 134217728 | bytes 14680064 | tf_op jit(solution)/shard_map/pallas_call | solution.py:359
  165.0 0.0 copy-done
  165.0 6.7 %shard_map.56 = f32[2048,128]{1,0:T(8,128)} custom-call(s32[4097]{0:T(1024)S(1)} %get-tuple-element.7.slots, f32[4096,128]{1,0:T(8,128)S(1)} %get-tuple-element.8.sums, f32[128,128]{1,0:T(8,128)S(1)} %copy-done), custom_call_target="tpu_custom_call" | custom-call | flops 402653184 | bytes 3145728 | tf_op jit(solution)/shard_map/pallas_call | solution.py:380
  (1 shorter events, 0.0 us)
Async XLA Ops:
  0.0 165.0 %copy-start = (f32[128,128]{1,0:T(8,128)S(1)}, f32[128,128]{1,0:T(8,128)}, u32[]{:S(2)}) copy-start(f32[128,128]{1,0:T(8,128)} %constant.7.clone.table) | copy-start | bytes 196612
  2.4 0.7 copy-start.1

commit v5 on v4

--- a/solution.py
+++ b/solution.py
@@ -235,6 +235,26 @@
     def place_of(group):
         return pl.ds(pl.multiple_of(group * group_rows, group_rows), group_rows)
 
+    def finish(group):
+        place = place_of(group)
+        taper = jnp.transpose(
+            jnp.broadcast_to(tapering[pl.ds(group, 1), :], (total.shape[1], group_rows))
+        )
+
+        @pl.when(me == 0)
+        def _():
+            leftward(group).wait_recv()
+            total[place, :] = (mine[place, :] + from_right[place, :]) * taper
+
+        @pl.when(me == last)
+        def _():
+            rightward(group).wait_recv()
+            total[place, :] = (mine[place, :] + from_left[place, :]) * taper
+
+        @pl.when((me > 0) & (me < last))
+        def _():
+            total[place, :] = (to_right[place, :] + from_right[place, :]) * taper
+
     def stage(step, carry):
         @pl.when(step < FLOWS)
         def _():
@@ -277,30 +297,17 @@
 
             leftward(left_group).start()
 
+        whole_group = step - LAG * last
+
+        @pl.when(whole_group >= 0)
+        def _():
+            finish(whole_group)
+
         return carry
 
     lax.fori_loop(0, FLOWS + LAG * last, stage, 0)
 
-    def finish(group, carry):
-        place = place_of(group)
-        taper = jnp.transpose(
-            jnp.broadcast_to(tapering[pl.ds(group, 1), :], (total.shape[1], group_rows))
-        )
-
-        @pl.when(me == 0)
-        def _():
-            leftward(group).wait_recv()
-            total[place, :] = (mine[place, :] + from_right[place, :]) * taper
-
-        @pl.when(me == last)
-        def _():
-            rightward(group).wait_recv()
-            total[place, :] = (mine[place, :] + from_left[place, :]) * taper
-
-        @pl.when((me > 0) & (me < last))
-        def _():
-            total[place, :] = (to_right[place, :] + from_right[place, :]) * taper
-
+    def settle(group, carry):
         @pl.when(me < last)
         def _():
             rightward(group).wait_send()
@@ -311,7 +318,7 @@
 
         return carry
 
-    lax.fori_loop(0, FLOWS, finish, 0)
+    lax.fori_loop(0, FLOWS, settle, 0)
     for number in range(count):
         far(number).wait_send()
         handed(number, own_piece(number)).wait_send()

time: 172 us -> 174 us (1.012)
  Pallas kernels: 169 us -> 171 us
    pallas_call x1, Pallas kernels: 162 us -> 164 us  [shards(): pl.pallas_call(functools.partial(exchange_kernel, lax.axis_size('chan'),...]
where the time goes in v5:
time: 174 us
  Pallas kernels  171 us (98%)
    pallas_call x1, Pallas kernels, shards(): pl.pallas_call(functools.partial(exchange_kernel, lax.axis_size('chan'),...  164 us
    pallas_call x1, Pallas kernels, shards(): pl.pallas_call(stack_kernel, out_shape=jax.ShapeDtypeStruct((capacity, le...  6.66 us

profile of v5, /device:TPU:0, one launch (start us, length us, event | category | flops | bytes accessed | tf_op | source)
XLA Modules:
  0.0 174.0 jit_solution(2303161689576457636)
XLA Ops:
  0.0 0.0 copy-start
  0.7 0.8 subtract_multiply_fusion
  1.5 0.9 fusion
  2.4 0.0 copy-start.1
  2.4 0.7 copy-done.1
  3.1 164.3 %shard_map.55 = (f32[4096,128]{1,0:T(8,128)S(1)}, s32[4097]{0:T(1024)S(1)}) custom-call(s32[4096]{0:T(1024)S(1)} %bitcast.5, s32[4096]{0:T(1024)S(1)} %add.3.receivers, s32[4096]{0:T(1024)S(1)} %copy-done.1, f32[32,128]{1,0:T(8,128)S(1)} %bitcast.6, bf16[512,32,128]{2,1,0:T(8,128)(2,1)} %own.1), custom_call_target="tpu_custom_call" | custom-call | flops 134217728 | bytes 14680064 | tf_op jit(solution)/shard_map/pallas_call | solution.py:366
  167.4 0.0 copy-done
  167.4 6.7 %shard_map.56 = f32[2048,128]{1,0:T(8,128)} custom-call(s32[4097]{0:T(1024)S(1)} %get-tuple-element.7.slots, f32[4096,128]{1,0:T(8,128)S(1)} %get-tuple-element.8.sums, f32[128,128]{1,0:T(8,128)S(1)} %copy-done), custom_call_target="tpu_custom_call" | custom-call | flops 402653184 | bytes 3145728 | tf_op jit(solution)/shard_map/pallas_call | solution.py:387
  (1 shorter events, 0.0 us)
Async XLA Ops:
  0.0 167.4 %copy-start = (f32[128,128]{1,0:T(8,128)S(1)}, f32[128,128]{1,0:T(8,128)}, u32[]{:S(2)}) copy-start(f32[128,128]{1,0:T(8,128)} %constant.7.clone.table) | copy-start | bytes 196612
  2.4 0.7 copy-start.1

commit v6 on v4

--- a/solution.py
+++ b/solution.py
@@ -15,7 +15,7 @@
 PIECES = 8
 DEPTH = 8
 FLOWS = 32
-LAG = 2
+LAG = 4
 MESH = pl.DeviceIdType.MESH
 
 

time: 172 us -> 167 us (0.971)
  Pallas kernels: 169 us -> 163 us
    pallas_call x1, Pallas kernels: 162 us -> 157 us  [shards(): pl.pallas_call(functools.partial(exchange_kernel, lax.axis_size('chan'),...]
where the time goes in v6:
time: 167 us
  Pallas kernels  163 us (98%)
    pallas_call x1, Pallas kernels, shards(): pl.pallas_call(functools.partial(exchange_kernel, lax.axis_size('chan'),...  157 us
    pallas_call x1, Pallas kernels, shards(): pl.pallas_call(stack_kernel, out_shape=jax.ShapeDtypeStruct((capacity, le...  6.66 us

profile of v6, /device:TPU:0, one launch (start us, length us, event | category | flops | bytes accessed | tf_op | source)
XLA Modules:
  0.0 166.5 jit_solution(10231359697410230509)
XLA Ops:
  0.0 0.0 copy-start
  0.7 0.8 subtract_multiply_fusion
  1.5 0.9 fusion
  2.4 0.0 copy-start.1
  2.4 0.7 copy-done.1
  3.1 156.8 %shard_map.55 = (f32[4096,128]{1,0:T(8,128)S(1)}, s32[4097]{0:T(1024)S(1)}) custom-call(s32[4096]{0:T(1024)S(1)} %bitcast.5, s32[4096]{0:T(1024)S(1)} %add.3.receivers, s32[4096]{0:T(1024)S(1)} %copy-done.1, f32[32,128]{1,0:T(8,128)S(1)} %bitcast.6, bf16[512,32,128]{2,1,0:T(8,128)(2,1)} %own.1), custom_call_target="tpu_custom_call" | custom-call | flops 134217728 | bytes 14680064 | tf_op jit(solution)/shard_map/pallas_call | solution.py:359
  159.9 0.0 copy-done
  159.9 6.7 %shard_map.56 = f32[2048,128]{1,0:T(8,128)} custom-call(s32[4097]{0:T(1024)S(1)} %get-tuple-element.7.slots, f32[4096,128]{1,0:T(8,128)S(1)} %get-tuple-element.8.sums, f32[128,128]{1,0:T(8,128)S(1)} %copy-done), custom_call_target="tpu_custom_call" | custom-call | flops 402653184 | bytes 3145728 | tf_op jit(solution)/shard_map/pallas_call | solution.py:380
  (1 shorter events, 0.0 us)
Async XLA Ops:
  0.0 159.9 %copy-start = (f32[128,128]{1,0:T(8,128)S(1)}, f32[128,128]{1,0:T(8,128)}, u32[]{:S(2)}) copy-start(f32[128,128]{1,0:T(8,128)} %constant.7.clone.table) | copy-start | bytes 196612
  2.4 0.7 copy-start.1
